TPU v7x, 32 devices: a whole 2x2x4 slice. The times are simulated.
32 devices in a mesh: slab: 4 (over z), curve: 8 (over y, x, core).
Axes of the slice: x: 2, y: 2, z: 4, core: 2. Of those that a mesh axis runs over, the one named last changes fastest.
Arguments:
- tracer_state: float32 [6, 125, 8192], P(None, None, ('slab', 'curve')), may hold values from -6 to 6
- inv_size: float32 [8192], P(('slab', 'curve')), may hold values from 1 to 6
- velocity: float32 [3, 6], replicated, may hold values from -1.5 to 1.5
- element_count: int32 [32], P(('slab', 'curve')), may hold values from 128 to 256, as said below
- face_kind: int32 [6, 8192], P(None, ('slab', 'curve')), may hold values from 0 to 5, as said below
- face_owner: int32 [6, 8192], P(None, ('slab', 'curve')), may hold values from 0 to 31, as said below
- face_index: int32 [6, 8192], P(None, ('slab', 'curve')), may hold values from 0 to 1535, as said below
- face_orient: int32 [6, 8192], P(None, ('slab', 'curve')), may hold values from 0 to 3
- hang_owner: int32 [4, 2048], P(None, ('slab', 'curve')), may hold values from 0 to 31, as said below
- hang_index: int32 [4, 2048], P(None, ('slab', 'curve')), may hold values from 0 to 1535, as said below
- hang_orient: int32 [4, 2048], P(None, ('slab', 'curve')), may hold values from 0 to 3
- mirror: int32 [32, 1024], P(('slab', 'curve')), may hold values from -1 to 1535, as said below
Outputs:
- new_state: float32 [6, 125, 8192], P(None, None, ('slab', 'curve'))
- increment: float32 [6, 125, 8192], P(None, None, ('slab', 'curve'))
Inputs may be any that keep to these rules, and one draw needn't show every extreme that they name: `element_count`: some device holds 256 live elements. `face_kind`: each device has exactly 64 sides of kind 5, whose face_index values are 0 to 63, each once. `face_owner`: A side of kind 5 has its own device as owner; every owner lies within 4 ranks of the device. `face_index`: for a remote owner the index is a slot below 128 that is filled in mirror; every filled slot to a device is named by exactly one side or hanging entry of that device. Local indices name faces of live elements. `hang_owner`: every owner lies within 4 ranks of the device. `hang_index`: same convention as face_index. `mirror`: filled entries name faces of live elements of the sender; columns whose destination lies outside the ranks are empty; some device receives all 128 slots filled from each of its 8 neighbours.
All inputs are finite; a program needn't handle non-finite values.
Results may differ from a plain program's by a relative error of at most 0.0003.
Values sent between devices are 32-bit elements; how exact they have to be, the bound alone decides.
A program may use at most 128 MiB of HBM per device.

v0:
```python
import functools
import math

import jax
import jax.numpy as jnp
import numpy as np
from jax import lax
from jax.experimental import pallas as pl
from jax.experimental.pallas import tpu as pltpu
from jax.sharding import PartitionSpec as P

NEAR = 4
B_ONE = 1432997174477.0 / 9575080441755.0
A_TWO = -567301805773.0 / 1357537059087.0
B_TWO = 5161836677717.0 / 13612068292357.0
COURANT = 0.3
MESH = pl.DeviceIdType.MESH
OFFSETS = tuple(range(-NEAR, 0)) + tuple(range(1, NEAR + 1))
PACK = 19
ROWS = 8 * PACK
HALF = ROWS + 8


def node_tables():
    points = np.array([-1.0, -math.sqrt(3.0 / 7.0), 0.0, math.sqrt(3.0 / 7.0), 1.0])
    weights = np.array([0.1, 49.0 / 90.0, 32.0 / 45.0, 49.0 / 90.0, 0.1])
    return (points, weights)


def lagrange_at(points, targets):
    values = np.ones((len(targets), len(points)))
    for column in range(len(points)):
        for another in range(len(points)):
            if another != column:
                values[:, column] *= (targets - points[another]) / (
                    points[column] - points[another]
                )
    return values


def derivative_table(points):
    count = len(points)
    scaled = [
        np.prod([points[c] - points[o] for o in range(count) if o != c]) for c in range(count)
    ]
    result = np.zeros((count, count))
    for r in range(count):
        for c in range(count):
            if r != c:
                result[r, c] = scaled[r] / scaled[c] / (points[r] - points[c])
        result[r, r] = sum(1.0 / (points[r] - points[o]) for o in range(count) if o != r)
    result[count // 2, count // 2] = 0.0
    return result


def tables():
    points, weights = node_tables()
    interp = lagrange_at(points, (points - 1.0) / 2.0)
    project = 0.5 * (interp.T * weights[None, :]) / weights[:, None]
    return interp, project, derivative_table(points)


INTERP, PROJECT, SLOPES = tables()


def combine(row, values):
    total = None
    for factor, value in zip(row, values):
        factor = float(factor)
        if abs(factor) < 1e-14:
            continue
        term = value if factor == 1.0 else factor * value
        total = term if total is None else total + term
    return total


def flipped(grid, first, second):
    half = [
        [grid[a][b] if a == 2 else jnp.where(first, grid[4 - a][b], grid[a][b]) for b in range(5)]
        for a in range(5)
    ]
    return [
        [half[a][b] if b == 2 else jnp.where(second, half[a][4 - b], half[a][b]) for b in range(5)]
        for a in range(5)
    ]


def mapped(grid, matrix):
    along = [
        [combine(matrix[a], [grid[i][b] for i in range(5)]) for b in range(5)] for a in range(5)
    ]
    return [
        [combine(matrix[b], [along[a][j] for j in range(5)]) for b in range(5)] for a in range(5)
    ]


def split_rows(block):
    block = jnp.concatenate([block, jnp.zeros((8, block.shape[1]), jnp.float32)], axis=0)
    high = block.astype(jnp.bfloat16)
    low = (block - high.astype(jnp.float32)).astype(jnp.bfloat16)
    return jnp.concatenate([high, low], axis=0)


def picked(parts, hot):
    both = jnp.dot(parts, hot, preferred_element_type=jnp.float32)
    return both[:ROWS] + both[HALF : HALF + ROWS]


def one_hot(index_row, depth):
    places = lax.broadcasted_iota(jnp.int32, (depth, index_row.shape[1]), 0)
    return jnp.where(places == index_row, 1.0, 0.0).astype(jnp.bfloat16)


def kernel(
    sizes,
    state,
    inv,
    vel,
    count,
    kind,
    owner,
    index,
    orient,
    hang_owner,
    hang_index,
    hang_orient,
    mirror,
    new_state,
    increment,
    middle,
    first,
    rate,
    packed,
    parts,
    hot_send,
    hot_local,
    hot_far,
    pick_local,
    pick_far,
    gathered,
    outside,
    outgoing,
    incoming,
    peak_curve,
    peak_slab,
    send_sem,
    recv_sem,
    curve_send,
    curve_recv,
    slab_send,
    slab_recv,
):
    n_slab, n_curve = sizes
    n_all = n_slab * n_curve
    slab, curve = lax.axis_index("slab"), lax.axis_index("curve")
    me = slab * n_curve + curve
    elements = state.shape[4]
    faces = 6 * elements
    slots = mirror.shape[1] // len(OFFSETS)

    def at(rank):
        return (rank // n_curve, rank % n_curve)

    def inside(rank):
        return jnp.logical_and(rank >= 0, rank < n_all)

    barrier = pltpu.get_barrier_semaphore()
    greeted = jnp.int32(n_curve + n_slab - 2)
    for offset in OFFSETS:
        other = me + offset
        greeted = greeted + inside(other).astype(jnp.int32)

        @pl.when(inside(other))
        def _():
            pl.semaphore_signal(barrier, inc=1, device_id=at(other), device_id_type=MESH)

    @pl.loop(1, n_curve)
    def _(k):
        pl.semaphore_signal(
            barrier, inc=1, device_id=(slab, (curve + k) % n_curve), device_id_type=MESH
        )

    @pl.loop(1, n_slab)
    def _(k):
        pl.semaphore_signal(
            barrier, inc=1, device_id=((slab + k) % n_slab, curve), device_id_type=MESH
        )

    for c in range(len(OFFSETS) // 2):
        hot_send[c] = one_hot(mirror[:, c * 2 * slots : (c + 1) * 2 * slots], faces)

    def pack_traces(source):
        def node(s, n):
            a, b = n // 5, n % 5
            end = 4 * (s % 2)
            if s < 2:
                return source[end, a, b]
            if s < 4:
                return source[a, end, b]
            return source[a, b, end]

        low_rows = lax.broadcasted_iota(jnp.int32, (8, elements), 0) < 6
        for s in range(6):
            cols = slice(s * elements, (s + 1) * elements)
            for n in range(PACK):
                value = node(s, n)
                if n < 18:
                    extra = node(s, PACK + n // 3)
                    j = n % 3
                    moved = pltpu.roll(extra, (6 - 2 * j) % 8, 0)
                    value = jnp.where(low_rows, value, moved)
                packed[8 * n : 8 * n + 8, cols] = value
        parts[...] = split_rows(packed[...])

    def copy(round_at, c):
        return pltpu.make_async_remote_copy(
            src_ref=outgoing.at[round_at, c],
            dst_ref=incoming.at[round_at, c],
            send_sem=send_sem.at[round_at, c],
            recv_sem=recv_sem.at[round_at, c],
            device_id=at(me + OFFSETS[c]),
            device_id_type=MESH,
        )

    def send_traces(round_at):
        for pair in (0, 3, 1, 2):
            block = picked(parts[...], hot_send[pair])
            outgoing[round_at, 2 * pair] = block[:, :slots]
            outgoing[round_at, 2 * pair + 1] = block[:, slots:]
            for c in (2 * pair, 2 * pair + 1):

                @pl.when(inside(me + OFFSETS[c]))
                def _():
                    copy(round_at, c).start()

    def await_traces(round_at):
        for c in range(len(OFFSETS)):

            @pl.when(inside(me - OFFSETS[c]))
            def _():
                copy(round_at, c).wait_recv()

            @pl.when(inside(me + OFFSETS[c]))
            def _():
                copy(round_at, c).wait_send()

    def local_part():
        @pl.loop(0, 7)
        def _(j):
            gathered[j] = picked(parts[...], hot_local[j])

    def far_part(round_at):
        block = jnp.concatenate(
            [incoming[round_at, c] for c in range(len(OFFSETS))], axis=1
        )
        far = split_rows(block)

        @pl.loop(0, 7)
        def _(j):
            gathered[j] += picked(far, hot_far[j])

    def volume_rate(source):
        scale = [-(vel[d] * inv[...]) for d in range(3)]
        for a in range(5):
            rate[a] = scale[0] * combine(SLOPES[a], [source[i] for i in range(5)])
        for b in range(5):
            rate[:, b] += scale[1] * combine(SLOPES[b], [source[:, i] for i in range(5)])
        for c in range(5):
            rate[:, :, c] += scale[2] * combine(SLOPES[c], [source[:, :, i] for i in range(5)])

    def nodes_of(j, cols):
        rows = lax.broadcasted_iota(jnp.int32, (8, cols.stop - cols.start), 0)

        def group(n):
            return gathered[j, 8 * n : 8 * n + 8, cols]

        nodes = [group(n) for n in range(PACK)]
        for k in range(6):
            base = 3 * k
            nodes.append(
                jnp.where(
                    rows < 2,
                    pltpu.roll(group(base), 2, 0),
                    jnp.where(
                        rows < 4,
                        pltpu.roll(group(base + 1), 4, 0),
                        pltpu.roll(group(base + 2), 6, 0),
                    ),
                )
            )
        return [[nodes[5 * a + b] for b in range(5)] for a in range(5)]

    def coarse_faces():
        entries = hang_orient.shape[1]
        turns = jnp.concatenate([hang_orient[c : c + 1] for c in range(4)], axis=1)
        children = lax.broadcasted_iota(jnp.int32, (1, 4 * entries), 1) // entries
        totals = None
        for half in range(2):
            cols = slice(half * 2 * entries, (half + 1) * 2 * entries)
            turn, child = turns[:, cols], children[:, cols]
            grid = nodes_of(6, cols)
            grid = flipped(
                grid,
                jnp.broadcast_to(((turn ^ child) & 1) == 1, (8, 2 * entries)),
                jnp.broadcast_to(((turn ^ child) & 2) == 2, (8, 2 * entries)),
            )
            grid = mapped(grid, PROJECT)
            grid = flipped(
                grid,
                jnp.broadcast_to((child & 1) == 1, (8, 2 * entries)),
                jnp.broadcast_to((child & 2) == 2, (8, 2 * entries)),
            )
            flat = [value for line in grid for value in line]
            totals = flat if totals is None else [x + y for x, y in zip(totals, flat)]
        return [x + pltpu.roll(x, entries, 1) for x in totals]

    def face_values():
        coarse = coarse_faces()
        for n in range(25):
            outside[3, n, :, 0:128] = coarse[n]
        for d in range(3):
            for half in range(elements // 128):
                cols = slice(half * 128, (half + 1) * 128)
                positive = vel[d, :, cols] > 0.0
                even, odd = nodes_of(2 * d, cols), nodes_of(2 * d + 1, cols)
                grid = [
                    [jnp.where(positive, even[a][b], odd[a][b]) for b in range(5)]
                    for a in range(5)
                ]

                def chosen(table):
                    return jnp.where(
                        positive, table[2 * d : 2 * d + 1, cols], table[2 * d + 1 : 2 * d + 2, cols]
                    )

                kinds, turns, places = chosen(kind), chosen(orient), chosen(index)
                fine = jnp.logical_and(kinds >= 1, kinds <= 4)
                child = jnp.where(fine, kinds - 1, 0)
                grid = flipped(
                    grid, ((turns ^ child) & 1) == 1, ((turns ^ child) & 2) == 2
                )
                finer = mapped(grid, INTERP)
                grid = [
                    [jnp.where(fine, finer[a][b], grid[a][b]) for b in range(5)] for a in range(5)
                ]
                grid = flipped(grid, (child & 1) == 1, (child & 2) == 2)
                is_coarse = kinds == 5
                place = jnp.where(is_coarse, places, 0)
                for n in range(25):
                    from_children = jnp.take_along_axis(
                        outside[3, n, :, 0:128], place, axis=1
                    )
                    outside[d, n, :, cols] = jnp.where(
                        is_coarse, from_children, grid[n // 5][n % 5]
                    )

    def face_rate(source):
        for d in range(3):
            positive = vel[d] > 0.0
            scale = -(jnp.abs(vel[d]) * (10.0 * inv[...]))

            def side(ref, end):
                return (ref.at[end], ref.at[:, end], ref.at[:, :, end])[d]

            around = outside[d].reshape(5, 5, 8, elements)
            inner = jnp.where(positive, side(source, 0)[...], side(source, 4)[...])
            flow = scale * (inner - around)
            side(rate, 0)[...] += jnp.where(positive, flow, 0.0)
            side(rate, 4)[...] += jnp.where(positive, 0.0, flow)

    live = lax.broadcasted_iota(jnp.int32, (1, elements), 1) < count[0]
    peak = jnp.max(jnp.where(live, inv[...], 0.0), axis=1, keepdims=True)
    peak_curve[0] = jnp.broadcast_to(peak, (8, 128))

    def curve_copy(k):
        return pltpu.make_async_remote_copy(
            src_ref=peak_curve.at[0],
            dst_ref=peak_curve.at[k],
            send_sem=curve_send.at[k],
            recv_sem=curve_recv.at[k],
            device_id=(slab, (curve + k) % n_curve),
            device_id_type=MESH,
        )

    def slab_copy(k):
        return pltpu.make_async_remote_copy(
            src_ref=peak_slab.at[0],
            dst_ref=peak_slab.at[k],
            send_sem=slab_send.at[k],
            recv_sem=slab_recv.at[k],
            device_id=((slab + k) % n_slab, curve),
            device_id_type=MESH,
        )

    pack_traces(state)
    pl.semaphore_wait(barrier, greeted)

    @pl.loop(1, n_curve)
    def _(k):
        curve_copy(k).start()

    send_traces(0)
    for c in range(len(OFFSETS)):

        @pl.when(jnp.logical_not(inside(me - OFFSETS[c])))
        def _():
            for round_at in range(2):
                incoming[round_at, c] = jnp.zeros((ROWS, slots), jnp.float32)

    def picks(owners, indices, usable):
        here = owners == me
        offset = me - owners
        column = jnp.where(offset < 0, offset + NEAR, offset + NEAR - 1)
        near = jnp.where(jnp.logical_and(usable, here), indices, -1)
        away = jnp.logical_and(usable, jnp.logical_not(here))
        return near, jnp.where(away, column * slots + indices, -1)

    near, away = picks(owner[...], index[...], kind[...] != 5)
    for s in range(6):
        pick_local[s] = near[s : s + 1]
        pick_far[s] = away[s : s + 1]
    near, away = picks(hang_owner[...], hang_index[...], hang_index[...] >= 0)
    pick_local[6] = jnp.concatenate([near[c : c + 1] for c in range(4)], axis=1)
    pick_far[6] = jnp.concatenate([away[c : c + 1] for c in range(4)], axis=1)

    @pl.loop(0, 7)
    def _(j):
        hot_local[j] = one_hot(pick_local[j], faces)

    @pl.loop(1, n_curve)
    def _(k):
        curve_copy(k).wait()

    peak_slab[0] = jnp.max(peak_curve[...], axis=0)

    @pl.loop(1, n_slab)
    def _(k):
        slab_copy(k).start()

    local_part()

    @pl.loop(0, 7)
    def _(j):
        hot_far[j] = one_hot(pick_far[j], slots * len(OFFSETS))

    volume_rate(state)

    @pl.loop(1, n_slab)
    def _(k):
        slab_copy(k).wait()

    peak_all = jnp.max(peak_slab[...], axis=0)
    step = COURANT / (peak_all * 16.0 * 1.5)
    step = jnp.concatenate([step] * (elements // 128), axis=1)

    await_traces(0)
    far_part(0)
    face_values()
    face_rate(state)
    for a in range(5):
        now = step * rate[a]
        first[a] = now
        middle[a] = state[a] + B_ONE * now

    pack_traces(middle)
    send_traces(1)
    local_part()
    volume_rate(middle)
    await_traces(1)
    far_part(1)
    face_values()
    face_rate(middle)
    for a in range(5):
        now = A_TWO * first[a] + step * rate[a]
        increment[a] = jnp.where(live, now, 0.0)
        new_state[a] = jnp.where(live, middle[a] + B_TWO * now, 0.0)


def per_device(sizes, tracer_state, inv_size, velocity, element_count, *rest):
    tracers, _, elements = tracer_state.shape
    hanging = rest[4].shape[1]
    slots = rest[7].shape[1] // len(OFFSETS)
    faces = 6 * elements
    state = jnp.pad(jnp.swapaxes(tracer_state, 0, 1), ((0, 0), (0, 8 - tracers), (0, 0)))
    state = state.reshape(5, 5, 5, 8, elements)
    vel = jnp.broadcast_to(
        jnp.pad(velocity, ((0, 0), (0, 8 - tracers)))[:, :, None], (3, 8, elements)
    )
    vmem = pl.BlockSpec(memory_space=pltpu.VMEM)
    smem = pl.BlockSpec(memory_space=pltpu.SMEM)
    grid_shape = (5, 5, 5, 8, elements)
    f32, bf16 = jnp.float32, jnp.bfloat16
    new_state, increment = pl.pallas_call(
        functools.partial(kernel, sizes),
        out_shape=[jax.ShapeDtypeStruct(grid_shape, f32)] * 2,
        in_specs=[vmem, vmem, vmem, smem] + [vmem] * 8,
        out_specs=[vmem, vmem],
        scratch_shapes=[
            pltpu.VMEM(grid_shape, f32),
            pltpu.VMEM(grid_shape, f32),
            pltpu.VMEM(grid_shape, f32),
            pltpu.VMEM((ROWS, faces), f32),
            pltpu.VMEM((2 * HALF, faces), bf16),
            pltpu.VMEM((len(OFFSETS) // 2, faces, 2 * slots), bf16),
            pltpu.VMEM((7, faces, elements), bf16),
            pltpu.VMEM((7, len(OFFSETS) * slots, elements), bf16),
            pltpu.VMEM((7, 1, elements), jnp.int32),
            pltpu.VMEM((7, 1, elements), jnp.int32),
            pltpu.VMEM((7, ROWS, elements), f32),
            pltpu.VMEM((4, 25, 8, elements), f32),
            pltpu.VMEM((2, len(OFFSETS), ROWS, slots), f32),
            pltpu.VMEM((2, len(OFFSETS), ROWS, slots), f32),
            pltpu.VMEM((sizes[1], 8, 128), f32),
            pltpu.VMEM((sizes[0], 8, 128), f32),
            pltpu.SemaphoreType.DMA((2, len(OFFSETS))),
            pltpu.SemaphoreType.DMA((2, len(OFFSETS))),
            pltpu.SemaphoreType.DMA((sizes[1],)),
            pltpu.SemaphoreType.DMA((sizes[1],)),
            pltpu.SemaphoreType.DMA((sizes[0],)),
            pltpu.SemaphoreType.DMA((sizes[0],)),
        ],
        compiler_params=pltpu.CompilerParams(
            collective_id=0, has_side_effects=True, vmem_limit_bytes=56 * 1024 * 1024
        ),
    )(state, inv_size.reshape(1, elements), vel, element_count, *rest)

    def back(block):
        return jnp.swapaxes(block.reshape(125, 8, elements)[:, :tracers], 0, 1)

    return back(new_state), back(increment)


def solution(mesh):
    both = ("slab", "curve")
    spread = P(None, both)
    in_specs = (P(None, None, both), P(both), P(), P(both)) + (spread,) * 7 + (P(both, None),)
    out_specs = (P(None, None, both), P(None, None, both))
    return jax.shard_map(
        functools.partial(per_device, (mesh.shape["slab"], mesh.shape["curve"])),
        mesh=mesh,
        in_specs=in_specs,
        out_specs=out_specs,
        check_vma=False,
    )
```

profile of v0, /device:TPU:28, one launch (start us, length us, event | category | flops | bytes accessed | tf_op | source)
XLA Modules:
  0.0 44.5 jit_solution(12863671326096912006)
XLA Ops:
  1.3 0.0 copy-start
  1.3 0.7 %copy-done = f32[3,6]{1,0:T(4,128)S(1)} copy-done((f32[3,6]{1,0:T(4,128)S(1)}, f32[3,6]{1,0:T(4,128)}, u32[]{:S(2)}) %copy-start) | copy-done | bytes 96
  2.0 0.7 %broadcast_in_dim.2.vel = f32[3,8,256]{2,1,0:T(8,128)} broadcast(f32[3,8]{1,0:T(4,128)S(1)} %pad.9), dimensions={0,1} | broadcast | bytes 24672 | tf_op jit(solution)/shard_map/broadcast_in_dim | solution.py:486
  2.6 1.6 %copy.19 = f32[125,6,256]{2,1,0:T(8,128)S(1)} copy(f32[125,6,256]{2,0,1:T(8,128)} %bitcast.14) | data formatting | bytes 1536000
  4.2 1.0 %pad.8.clone = f32[125,8,256]{2,1,0:T(8,128)} pad(f32[125,6,256]{2,1,0:T(8,128)S(1)} %copy.19, f32[]{:T(128)} %constant.2.clone.1), padding=0_0x0_2x0_0 | pad | bytes 1792004 | tf_op jit(solution)/shard_map/jit(_pad)/pad | solution.py:484
  5.3 36.0 %shard_map.131 = (f32[5,5,5,8,256]{4,3,2,1,0:T(8,128)}, f32[5,5,5,8,256]{4,3,2,1,0:T(8,128)}) custom-call(f32[5,5,5,8,256]{4,3,2,1,0:T(8,128)} %bitcast.11, f32[1,256]{1,0:T(1,128)} %bitcast.15, f32[3,8,256]{2,1,0:T(8,128)} %broadcast_in_dim.2.vel, s32[1]{0:T(128)S(6)} %copy.22.count, s32[6,256]{1,0:T(8,128)} %kind.1, s32[6,256]{1,0:T(8,128)} %owner.1, ...), custom_call_target="tpu_custom_call" | custom-call | tf_op jit(solution)/shard_map/pallas_call | solution.py:493
  41.3 3.1 %copy_bitcast_fusion = (f32[6,125,256]{2,1,0:T(8,128)}, f32[6,125,256]{2,1,0:T(8,128)}) fusion(f32[125,6,256]{2,1,0:T(8,128)} %bitcast.13, f32[125,6,256]{2,1,0:T(8,128)} %bitcast.12), kind=kLoop, calls=%fused_computation | loop fusion | bytes 3072000 | tf_op jit(solution)/shard_map/transpose | solution.py:528
  (1 shorter events, 0.0 us)
Async XLA Ops:
  1.3 0.7 %copy-start = (f32[3,6]{1,0:T(4,128)S(1)}, f32[3,6]{1,0:T(4,128)}, u32[]{:S(2)}) copy-start(f32[3,6]{1,0:T(4,128)} %param.14) | copy-start | bytes 220
where the time goes:
time: 44.7 us; the launch traced here: 44.5 us
  Pallas kernels  36 us (81%)
  local copies, waits for them, and re-layouts  7.13 us (16%)
  between operations  1.3 us (3%)
    pallas_call x1, Pallas kernels, per_device(): pl.pallas_call(functools.partial(kernel, sizes), out_shape=[jax.ShapeDtyp...  36 us
    transpose x1, local copies, waits for them, and re-layouts, back(): return jnp.swapaxes(block.reshape(125, 8, elements)[:, :tracers], 0, 1)  3.13 us
    unnamed x3, local copies, waits for them, and re-layouts  2.27 us
    pad x1, local copies, waits for them, and re-layouts, per_device(): jnp.pad(jnp.swapaxes(tracer_state, 0, 1), ((0, 0), (0, 8 - tracers), (0,...  1.04 us

commit v1 on v0

--- a/solution.py
+++ b/solution.py
@@ -115,7 +115,7 @@
     sizes,
     state,
     inv,
-    vel,
+    speeds,
     count,
     kind,
     owner,
@@ -139,6 +139,7 @@
     pick_far,
     gathered,
     outside,
+    vel,
     outgoing,
     incoming,
     peak_curve,
@@ -186,6 +187,13 @@
             barrier, inc=1, device_id=((slab + k) % n_slab, curve), device_id_type=MESH
         )
 
+    tracer_row = lax.broadcasted_iota(jnp.int32, (8, elements), 0)
+    for d in range(3):
+        line = jnp.zeros((8, elements), jnp.float32)
+        for t in range(speeds.shape[1]):
+            line = jnp.where(tracer_row == t, speeds[d, t], line)
+        vel[d] = line
+
     for c in range(len(OFFSETS) // 2):
         hot_send[c] = one_hot(mirror[:, c * 2 * slots : (c + 1) * 2 * slots], faces)
 
@@ -233,12 +241,8 @@
                 def _():
                     copy(round_at, c).start()
 
-    def await_traces(round_at):
+    def await_sent(round_at):
         for c in range(len(OFFSETS)):
-
-            @pl.when(inside(me - OFFSETS[c]))
-            def _():
-                copy(round_at, c).wait_recv()
 
             @pl.when(inside(me + OFFSETS[c]))
             def _():
@@ -250,14 +254,23 @@
             gathered[j] = picked(parts[...], hot_local[j])
 
     def far_part(round_at):
-        block = jnp.concatenate(
-            [incoming[round_at, c] for c in range(len(OFFSETS))], axis=1
-        )
-        far = split_rows(block)
-
-        @pl.loop(0, 7)
-        def _(j):
-            gathered[j] += picked(far, hot_far[j])
+        for pair in (1, 2, 0, 3):
+            for c in (2 * pair, 2 * pair + 1):
+
+                @pl.when(inside(me - OFFSETS[c]))
+                def _():
+                    copy(round_at, c).wait_recv()
+
+            far = split_rows(
+                jnp.concatenate(
+                    [incoming[round_at, 2 * pair], incoming[round_at, 2 * pair + 1]], axis=1
+                )
+            )
+
+            @pl.loop(0, 7)
+            def _(j):
+                rows = slice(2 * pair * slots, 2 * (pair + 1) * slots)
+                gathered[j] += picked(far, hot_far[j, rows, :])
 
     def volume_rate(source):
         scale = [-(vel[d] * inv[...]) for d in range(3)]
@@ -453,7 +466,6 @@
     step = COURANT / (peak_all * 16.0 * 1.5)
     step = jnp.concatenate([step] * (elements // 128), axis=1)
 
-    await_traces(0)
     far_part(0)
     face_values()
     face_rate(state)
@@ -466,7 +478,6 @@
     send_traces(1)
     local_part()
     volume_rate(middle)
-    await_traces(1)
     far_part(1)
     face_values()
     face_rate(middle)
@@ -474,6 +485,8 @@
         now = A_TWO * first[a] + step * rate[a]
         increment[a] = jnp.where(live, now, 0.0)
         new_state[a] = jnp.where(live, middle[a] + B_TWO * now, 0.0)
+    await_sent(0)
+    await_sent(1)
 
 
 def per_device(sizes, tracer_state, inv_size, velocity, element_count, *rest):
@@ -483,9 +496,6 @@
     faces = 6 * elements
     state = jnp.pad(jnp.swapaxes(tracer_state, 0, 1), ((0, 0), (0, 8 - tracers), (0, 0)))
     state = state.reshape(5, 5, 5, 8, elements)
-    vel = jnp.broadcast_to(
-        jnp.pad(velocity, ((0, 0), (0, 8 - tracers)))[:, :, None], (3, 8, elements)
-    )
     vmem = pl.BlockSpec(memory_space=pltpu.VMEM)
     smem = pl.BlockSpec(memory_space=pltpu.SMEM)
     grid_shape = (5, 5, 5, 8, elements)
@@ -493,7 +503,7 @@
     new_state, increment = pl.pallas_call(
         functools.partial(kernel, sizes),
         out_shape=[jax.ShapeDtypeStruct(grid_shape, f32)] * 2,
-        in_specs=[vmem, vmem, vmem, smem] + [vmem] * 8,
+        in_specs=[vmem, vmem, smem, smem] + [vmem] * 8,
         out_specs=[vmem, vmem],
         scratch_shapes=[
             pltpu.VMEM(grid_shape, f32),
@@ -508,6 +518,7 @@
             pltpu.VMEM((7, 1, elements), jnp.int32),
             pltpu.VMEM((7, ROWS, elements), f32),
             pltpu.VMEM((4, 25, 8, elements), f32),
+            pltpu.VMEM((3, 8, elements), f32),
             pltpu.VMEM((2, len(OFFSETS), ROWS, slots), f32),
             pltpu.VMEM((2, len(OFFSETS), ROWS, slots), f32),
             pltpu.VMEM((sizes[1], 8, 128), f32),
@@ -522,7 +533,7 @@
         compiler_params=pltpu.CompilerParams(
             collective_id=0, has_side_effects=True, vmem_limit_bytes=56 * 1024 * 1024
         ),
-    )(state, inv_size.reshape(1, elements), vel, element_count, *rest)
+    )(state, inv_size.reshape(1, elements), velocity, element_count, *rest)
 
     def back(block):
         return jnp.swapaxes(block.reshape(125, 8, elements)[:, :tracers], 0, 1)

time: 44.7 us -> 47.5 us (1.063)
  the two profiles are of different devices: /device:TPU:28 before, /device:TPU:13 now
where the time goes in v1:
time: 47.5 us; the launch traced here: 47.3 us
  Pallas kernels  40.2 us (85%)
  local copies, waits for them, and re-layouts  5.77 us (12%)
  between operations  1.29 us (3%)
    pallas_call x1, Pallas kernels, per_device(): pl.pallas_call(functools.partial(kernel, sizes), out_shape=[jax.ShapeDtyp...  40.2 us
    transpose x1, local copies, waits for them, and re-layouts, back(): return jnp.swapaxes(block.reshape(125, 8, elements)[:, :tracers], 0, 1)  3.13 us
    unnamed x1, local copies, waits for them, and re-layouts  1.6 us
    pad x1, local copies, waits for them, and re-layouts, per_device(): jnp.pad(jnp.swapaxes(tracer_state, 0, 1), ((0, 0), (0, 8 - tracers), (0,...  1.05 us

profile of v1, /device:TPU:13, one launch (start us, length us, event | category | flops | bytes accessed | tf_op | source)
XLA Modules:
  0.0 47.3 jit_solution(9814746186945488725)
XLA Ops:
  1.3 1.6 %copy.19 = f32[125,6,256]{2,1,0:T(8,128)S(1)} copy(f32[125,6,256]{2,0,1:T(8,128)} %bitcast.14) | data formatting | bytes 1536000
  2.9 1.0 %pad.4.clone = f32[125,8,256]{2,1,0:T(8,128)} pad(f32[125,6,256]{2,1,0:T(8,128)S(1)} %copy.19, f32[]{:T(128)} %constant.2.clone.1), padding=0_0x0_2x0_0 | pad | bytes 1792004 | tf_op jit(solution)/shard_map/jit(_pad)/pad | solution.py:497
  3.9 40.2 %shard_map.131 = (f32[5,5,5,8,256]{4,3,2,1,0:T(8,128)}, f32[5,5,5,8,256]{4,3,2,1,0:T(8,128)}) custom-call(f32[5,5,5,8,256]{4,3,2,1,0:T(8,128)} %bitcast.11, f32[1,256]{1,0:T(1,128)} %bitcast.15, f32[3,6]{1,0:T(4,128)} %speeds.1, s32[1]{0:T(128)S(6)} %copy.22.count, s32[6,256]{1,0:T(8,128)} %kind.1, s32[6,256]{1,0:T(8,128)} %owner.1, s32[6,256]{1,0:T(8,128)} %index.1, ...), custom_call_target="tpu_custom_call" | custom-call | tf_op jit(solution)/shard_map/pallas_call | solution.py:503
  44.1 3.1 %copy_bitcast_fusion = (f32[6,125,256]{2,1,0:T(8,128)}, f32[6,125,256]{2,1,0:T(8,128)}) fusion(f32[125,6,256]{2,1,0:T(8,128)} %bitcast.13, f32[125,6,256]{2,1,0:T(8,128)} %bitcast.12), kind=kLoop, calls=%fused_computation | loop fusion | bytes 3072000 | tf_op jit(solution)/shard_map/transpose | solution.py:539
